TPU v7x, 32 devices: a whole 2x2x4 slice. The times are simulated.
32 devices in a mesh: dp: 8 (over z, core), tensor: 4 (over y, x).
Axes of the slice: x: 2, y: 2, z: 4, core: 2. Of those that a mesh axis runs over, the one named last changes fastest.
Arguments:
- tokens_in: bfloat16 [8192, 1024], P('dp'), may hold values from -6 to 6
- norm_params: float32 [4, 1024], replicated, may hold values from -1.2 to 3.6
- query_key_value_weight: bfloat16 [3, 1024, 1024], P(None, None, 'tensor'), may hold values from -0.09375 to 0.09375
- out_weight: bfloat16 [1024, 1024], P('tensor'), may hold values from -1.5 to 1.5
- fc_weight: bfloat16 [1024, 4096], P(None, 'tensor'), may hold values from -0.1875 to 0.1875
- proj_weight: bfloat16 [4096, 1024], P('tensor'), may hold values from -0.09375 to 0.09375
- factors: float32 [4, 4, 1024], replicated, may hold values from -0.12 to 0.12
- first_moment: float32 [4, 4, 1024], replicated, may hold values from -0.375 to 0.375
- second_moment: float32 [4, 4, 1024], replicated, may hold values from 0.015625 to 0.0625
- grad_out: bfloat16 [8192, 1024], P('dp'), may hold values from -6 to 6
Outputs:
- block_out: bfloat16 [8192, 1024], P(('dp', 'tensor'))
- input_grad: float32 [8192, 1024], P(('dp', 'tensor'))
- clipped_grad: float32 [4, 4, 1024], replicated
- grad_norm: float32 [], replicated
- factors_new: float32 [4, 4, 1024], replicated
- first_new: float32 [4, 4, 1024], replicated
- second_new: float32 [4, 4, 1024], replicated
All inputs are finite; a program needn't handle non-finite values.
Results may differ from a plain program's by a relative error of at most 0.015.
Values may be sent and summed in bfloat16 or wider, within the bound.
A program may use at most 128 MiB of HBM per device.

v0:
```python
import jax
import jax.numpy as jnp
from jax import lax
from jax.sharding import PartitionSpec as P

HD = 64
SEQ = 1024
STEP = 5


EPSILON = 1e-05
ADAPTER_SCALING = 8.0
CLIP_NORM = 16.0
LEARN_RATE = 0.03
BETA_ONE = 0.5
BETA_TWO = 0.5
WEIGHT_DECAY = 0.01
ADAM_EPSILON = 1e-08
NEG_LARGE = -1e30


def matrix_product(left, right):
    return jnp.dot(left, right, preferred_element_type=jnp.float32)


def product_with_transpose(left, right):
    return lax.dot_general(
        left, right, (((1,), (1,)), ((), ())), preferred_element_type=jnp.float32
    )


def transpose_then_product(left, right):
    return lax.dot_general(
        left, right, (((0,), (0,)), ((), ())), preferred_element_type=jnp.float32
    )


def normalize(value_rows_local, gain_vec, bias_vec):
    centered = value_rows_local - jnp.mean(value_rows_local, -1, keepdims=True)
    inverse = lax.rsqrt(jnp.mean(centered * centered, -1, keepdims=True) + EPSILON)
    unit_rows = centered * inverse
    return (unit_rows * gain_vec + bias_vec, unit_rows, inverse)


def normalize_back(incoming, unit_rows, inverse, gain_vec):
    scaled = incoming * gain_vec
    return inverse * (
        scaled
        - jnp.mean(scaled, -1, keepdims=True)
        - unit_rows * jnp.mean(scaled * unit_rows, -1, keepdims=True)
    )


def causal_scores(query_block, key_all, block_index, block_len):
    scores = (
        jnp.einsum("bqhd,bkhd->bhqk", query_block, key_all, preferred_element_type=jnp.float32)
        * 0.125
    )
    query_pos = block_index * block_len + jnp.arange(block_len)
    allowed = jnp.arange(SEQ)[None, :] <= query_pos[:, None]
    return jnp.where(allowed, scores, NEG_LARGE)


def attention_forward(query_rows_local, key_all, value_all):
    block_len = min(512, SEQ)
    outputs = []
    logsums = []
    for block_index in range(SEQ // block_len):
        query_block = query_rows_local[:, block_index * block_len : (block_index + 1) * block_len]
        scores = causal_scores(query_block, key_all, block_index, block_len)
        row_max = jnp.max(scores, -1, keepdims=True)
        exponent = jnp.exp(scores - row_max)
        row_total = jnp.sum(exponent, -1, keepdims=True)
        probability = (exponent / row_total).astype(jnp.bfloat16)
        mixture = jnp.einsum(
            "bhqk,bkhd->bqhd", probability, value_all, preferred_element_type=jnp.float32
        )
        outputs.append(mixture.astype(jnp.bfloat16))
        logsums.append(row_max[..., 0] + jnp.log(row_total[..., 0]))
    return (jnp.concatenate(outputs, 1), jnp.concatenate(logsums, 2))


def attention_backward(query_rows_local, key_all, value_all, grad_mixture, logsums):
    block_len = min(512, SEQ)
    grad_queries = []
    grad_keys = jnp.zeros(key_all.shape, jnp.float32)
    value_gradient_rows = jnp.zeros(value_all.shape, jnp.float32)
    for block_index in range(SEQ // block_len):
        lower = block_index * block_len
        query_block = query_rows_local[:, lower : lower + block_len]
        grad_block = grad_mixture[:, lower : lower + block_len]
        scores = causal_scores(query_block, key_all, block_index, block_len)
        probability = jnp.exp(scores - logsums[:, :, lower : lower + block_len, None])
        grad_prob = jnp.einsum(
            "bqhd,bkhd->bhqk", grad_block, value_all, preferred_element_type=jnp.float32
        )
        row_delta = jnp.sum(grad_prob * probability, -1, keepdims=True)
        dscore = (0.125 * (probability * (grad_prob - row_delta))).astype(jnp.bfloat16)
        grad_queries.append(
            jnp.einsum(
                "bhqk,bkhd->bqhd", dscore, key_all, preferred_element_type=jnp.float32
            ).astype(jnp.bfloat16)
        )
        grad_keys = grad_keys + jnp.einsum(
            "bhqk,bqhd->bkhd", dscore, query_block, preferred_element_type=jnp.float32
        )
        value_gradient_rows = value_gradient_rows + jnp.einsum(
            "bhqk,bqhd->bkhd",
            probability.astype(jnp.bfloat16),
            grad_block,
            preferred_element_type=jnp.float32,
        )
    return (
        jnp.concatenate(grad_queries, 1),
        grad_keys.astype(jnp.bfloat16),
        value_gradient_rows.astype(jnp.bfloat16),
    )


def adam_step(factor_grad, weights, first_old, second_old, grad_norm):
    clipped = factor_grad * (CLIP_NORM / jnp.maximum(grad_norm, CLIP_NORM))
    first_new = BETA_ONE * first_old + (1.0 - BETA_ONE) * clipped
    second_new = BETA_TWO * second_old + (1.0 - BETA_TWO) * clipped * clipped
    first_hat = first_new / (1.0 - BETA_ONE**STEP)
    second_hat = second_new / (1.0 - BETA_TWO**STEP)
    weights_new = weights - LEARN_RATE * (
        first_hat / (jnp.sqrt(second_hat) + ADAM_EPSILON) + WEIGHT_DECAY * weights
    )
    return (clipped, weights_new, first_new, second_new)


def body(
    tokens_in,
    norm_params,
    query_key_value_weight,
    out_weight,
    fc_weight,
    proj_weight,
    factors,
    first_moment,
    second_moment,
    grad_out,
):
    tensor_size = lax.axis_size("tensor")
    tensor_rank = lax.axis_index("tensor")
    token_count = tokens_in.shape[0]
    doc_count = token_count // SEQ
    local_width = query_key_value_weight.shape[2]
    heads_here = local_width // HD
    row_count = token_count // tensor_size
    row_start = tensor_rank * row_count
    rank_count = factors.shape[1]
    full_width = factors.shape[2]
    inputs = tokens_in.astype(jnp.float32)
    first_normalized, unit_one, inverse_one = normalize(inputs, norm_params[0], norm_params[1])
    first_normalized_reduced = first_normalized.astype(jnp.bfloat16)
    factor_reduced_precision = factors.astype(jnp.bfloat16)
    column_offset = tensor_rank * local_width
    query_adapter_output = lax.dynamic_slice_in_dim(
        factor_reduced_precision[1], column_offset, local_width, 1
    )
    value_adapter_output = lax.dynamic_slice_in_dim(
        factor_reduced_precision[3], column_offset, local_width, 1
    )
    query_down_factor = product_with_transpose(
        first_normalized_reduced, factor_reduced_precision[0]
    ).astype(jnp.bfloat16)
    value_down_factor = product_with_transpose(
        first_normalized_reduced, factor_reduced_precision[2]
    ).astype(jnp.bfloat16)
    query_rows_local = (
        matrix_product(first_normalized_reduced, query_key_value_weight[0])
        + ADAPTER_SCALING * matrix_product(query_down_factor, query_adapter_output)
    ).astype(jnp.bfloat16)
    keys_low = matrix_product(first_normalized_reduced, query_key_value_weight[1]).astype(
        jnp.bfloat16
    )
    values_low = (
        matrix_product(first_normalized_reduced, query_key_value_weight[2])
        + ADAPTER_SCALING * matrix_product(value_down_factor, value_adapter_output)
    ).astype(jnp.bfloat16)
    head_shape = (doc_count, SEQ, heads_here, HD)
    query_heads = query_rows_local.reshape(head_shape)
    keys_heads = keys_low.reshape(head_shape)
    values_heads = values_low.reshape(head_shape)
    mixture, logsums = attention_forward(query_heads, keys_heads, values_heads)
    attn_part = matrix_product(mixture.reshape(token_count, local_width), out_weight)
    grad_full = grad_out.astype(jnp.float32)
    attn_rows = lax.psum_scatter(
        attn_part.astype(jnp.bfloat16), "tensor", scatter_dimension=0, tiled=True
    ).astype(jnp.float32)
    resid_rows = lax.dynamic_slice_in_dim(inputs, row_start, row_count, 0) + attn_rows
    normed_two_rows, unit_two, inverse_two = normalize(resid_rows, norm_params[2], norm_params[3])
    normed_two_low = lax.all_gather(
        normed_two_rows.astype(jnp.bfloat16), "tensor", axis=0, tiled=True
    )
    hidden_pre = matrix_product(normed_two_low, fc_weight)
    hidden_act, gelu_pull = jax.vjp(
        lambda argument: jax.nn.gelu(argument, approximate=True), hidden_pre
    )
    mlp_part = matrix_product(hidden_act.astype(jnp.bfloat16), proj_weight)
    grad_hidden = product_with_transpose(grad_out, proj_weight)
    grad_pre = gelu_pull(grad_hidden)[0].astype(jnp.bfloat16)
    second_part = product_with_transpose(grad_pre, fc_weight)
    out_rows = resid_rows + lax.psum_scatter(
        mlp_part.astype(jnp.bfloat16), "tensor", scatter_dimension=0, tiled=True
    ).astype(jnp.float32)
    second_rows = lax.psum_scatter(
        second_part.astype(jnp.bfloat16), "tensor", scatter_dimension=0, tiled=True
    ).astype(jnp.float32)
    resid_grad_rows = lax.dynamic_slice_in_dim(grad_full, row_start, row_count, 0) + normalize_back(
        second_rows, unit_two, inverse_two, norm_params[2]
    )
    resid_grad_low = lax.all_gather(
        resid_grad_rows.astype(jnp.bfloat16), "tensor", axis=0, tiled=True
    )
    grad_mixture = product_with_transpose(resid_grad_low, out_weight).astype(jnp.bfloat16)
    query_gradient, grad_keys, value_gradient_rows = attention_backward(
        query_heads, keys_heads, values_heads, grad_mixture.reshape(head_shape), logsums
    )
    query_gradient = query_gradient.reshape(token_count, local_width)
    grad_keys = grad_keys.reshape(token_count, local_width)
    value_gradient_rows = value_gradient_rows.reshape(token_count, local_width)
    stacked = jnp.stack((query_gradient, grad_keys, value_gradient_rows))
    first_part = jnp.einsum(
        "stc,sdc->td", stacked, query_key_value_weight, preferred_element_type=jnp.float32
    )
    query_up_factor = ADAPTER_SCALING * product_with_transpose(query_gradient, query_adapter_output)
    value_up_factor = ADAPTER_SCALING * product_with_transpose(
        value_gradient_rows, value_adapter_output
    )
    first_part = first_part + jnp.dot(
        query_up_factor,
        factor_reduced_precision[0].astype(jnp.float32),
        precision=lax.Precision.HIGHEST,
    )
    first_part = first_part + jnp.dot(
        value_up_factor,
        factor_reduced_precision[2].astype(jnp.float32),
        precision=lax.Precision.HIGHEST,
    )
    first_rows = lax.psum_scatter(
        first_part.astype(jnp.bfloat16), "tensor", scatter_dimension=0, tiled=True
    ).astype(jnp.float32)
    unit_rows = lax.dynamic_slice_in_dim(unit_one, row_start, row_count, 0)
    inverse_rows = lax.dynamic_slice_in_dim(inverse_one, row_start, row_count, 0)
    input_rows = resid_grad_rows + normalize_back(
        first_rows, unit_rows, inverse_rows, norm_params[0]
    )
    query_cross_term = transpose_then_product(query_gradient, first_normalized_reduced)
    value_cross_term = transpose_then_product(value_gradient_rows, first_normalized_reduced)
    query_down_gradient = ADAPTER_SCALING * jnp.dot(
        query_adapter_output.astype(jnp.float32), query_cross_term, precision=lax.Precision.HIGHEST
    )
    value_down_gradient = ADAPTER_SCALING * jnp.dot(
        value_adapter_output.astype(jnp.float32), value_cross_term, precision=lax.Precision.HIGHEST
    )
    empty_slot = jnp.zeros((rank_count, full_width), jnp.float32)
    up_grad_query = lax.dynamic_update_slice_in_dim(
        empty_slot,
        ADAPTER_SCALING * transpose_then_product(query_down_factor, query_gradient),
        column_offset,
        1,
    )
    up_grad_value = lax.dynamic_update_slice_in_dim(
        empty_slot,
        ADAPTER_SCALING * transpose_then_product(value_down_factor, value_gradient_rows),
        column_offset,
        1,
    )
    partial_grad = jnp.stack(
        (query_down_gradient, up_grad_query, value_down_gradient, up_grad_value)
    )
    reduced = lax.psum(partial_grad, ("dp", "tensor"))
    grad_norm = jnp.sqrt(jnp.sum(reduced * reduced))
    clipped, weights_new, first_new, second_new = adam_step(
        reduced, factors, first_moment, second_moment, grad_norm
    )
    return (
        out_rows.astype(jnp.bfloat16),
        input_rows,
        clipped,
        grad_norm,
        weights_new,
        first_new,
        second_new,
    )


def solution(mesh):
    placed = (
        P("dp", None),
        P(),
        P(None, None, "tensor"),
        P("tensor", None),
        P(None, "tensor"),
        P("tensor", None),
        P(),
        P(),
        P(),
        P("dp", None),
    )
    return jax.shard_map(
        body,
        mesh=mesh,
        in_specs=placed,
        out_specs=(P(("dp", "tensor"), None), P(("dp", "tensor"), None), P(), P(), P(), P(), P()),
        check_vma=False,
    )
```

profile of v0, /device:TPU:1, one launch (start us, length us, event | category | flops | bytes accessed | tf_op | source)
XLA Modules:
  0.0 518.2 jit_solution(9542759216489154347)
XLA Ops:
  10.2 2.3 multiply_reduce_fusion.2
  12.6 2.9 subtract_multiply_fusion
  24.2 2.9 fusion.6
  28.9 13.6 %fusion.4 = f32[4,512]{1,0:T(4,128)S(1)} fusion(f32[4,512,1024]{2,1,0:T(8,128)S(1)} %get-tuple-element.31, f32[4,512]{1,0:T(4,128)S(1)} %get-tuple-element.30, pred[512,1024]{1,0:T(8,128)(4,1)S(1)} %iota_compare_fusion.1), kind=kLoop, calls=%fused_computation.16 | loop fusion | flops 8386560 | bytes 8929280 | tf_op jit(solution)/shard_map/reduce_sum | solution.py:73
  42.9 2.9 fusion.121
  45.8 2.3 fusion.5
  48.2 2.9 fusion.122
  53.4 4.0 convert_element_type.151
  57.4 33.4 %reduce-scatter.5.cloned.1.call-done = bf16[256,1024]{1,0:T(8,128)(2,1)} async-done(((bf16[1024,1024]{1,0:T(8,128)(2,1)}), bf16[256,1024]{1,0:T(8,128)(2,1)}) %reduce-scatter.5.cloned.1.call-update) | async-done | bytes 524304 | tf_op jit(solution)/shard_map/reduce_scatter | solution.py:189
  93.8 35.4 %all-gather.3.cloned.1.call-done = bf16[1024,1024]{1,0:T(8,128)(2,1)} async-done(((bf16[256,1024]{1,0:T(8,128)(2,1)}), bf16[1024,1024]{1,0:T(8,128)(2,1)}) %all-gather.3.cloned.1.call-update) | async-done | bytes 2097168 | tf_op jit(solution)/shard_map/all_gather | solution.py:194
  129.2 5.8 %fusion.198 = f32[1024,1024]{1,0:T(8,128)} fusion(bf16[1024,1024]{1,0:T(8,128)(2,1)} %all-gather.3.cloned.1.call-done, bf16[1024,1024]{1,0:T(8,128)(2,1)S(1)} %copy-done), kind=kOutput, calls=%fused_computation.212 | convolution fusion | flops 2147483648 | bytes 8388608 | tf_op jit(solution)/shard_map/dot_general | solution.py:23
  135.0 9.3 %fusion.82 = bf16[1024,1024]{1,0:T(8,128)(2,1)} fusion(bf16[1024,1024]{1,0:T(8,128)(2,1)S(1)} %copy-done, f32[1024,1024]{1,0:T(8,128)} %fusion.198, bf16[1024,1024]{1,0:T(8,128)(2,1)} %param.19, bf16[1024,1024]{1,0:T(8,128)(2,1)} %param.15), kind=kOutput, calls=%fused_computation.73 | convolution fusion | flops 4316987392 | bytes 12582912 | tf_op jit(solution)/shard_map/dot_general | solution.py:27
  144.4 6.9 %fusion.85 = bf16[1024,1024]{1,0:T(8,128)(2,1)} fusion(bf16[1024,1024]{1,0:T(8,128)(2,1)} %param.15, f32[1024,1024]{1,0:T(8,128)} %fusion.198), kind=kOutput, calls=%fused_computation.74 | convolution fusion | flops 2157969408 | bytes 8388608 | tf_op jit(solution)/shard_map/dot_general | solution.py:23
  151.4 28.4 %reduce-scatter.9.cloned.1.call-done = bf16[256,1024]{1,0:T(8,128)(2,1)} async-done(((bf16[1024,1024]{1,0:T(8,128)(2,1)}), bf16[256,1024]{1,0:T(8,128)(2,1)}) %reduce-scatter.9.cloned.1.call-update) | async-done | bytes 524304 | tf_op jit(solution)/shard_map/reduce_scatter | solution.py:208
  181.1 36.7 %reduce-scatter.7.cloned.1.call-done = bf16[256,1024]{1,0:T(8,128)(2,1)} async-done(((bf16[1024,1024]{1,0:T(8,128)(2,1)}), bf16[256,1024]{1,0:T(8,128)(2,1)}) %reduce-scatter.7.cloned.1.call-update) | async-done | bytes 524304 | tf_op jit(solution)/shard_map/reduce_scatter | solution.py:205
  217.8 3.2 fusion.192
  221.1 35.4 %all-gather.5.cloned.1.call-done = bf16[1024,1024]{1,0:T(8,128)(2,1)} async-done(((bf16[256,1024]{1,0:T(8,128)(2,1)}), bf16[1024,1024]{1,0:T(8,128)(2,1)}) %all-gather.5.cloned.1.call-update) | async-done | bytes 2097168 | tf_op jit(solution)/shard_map/all_gather | solution.py:214
  256.5 2.3 convolution_convert_fusion.1
  258.8 4.5 fusion.141
  263.3 4.5 fusion.142
  267.8 22.2 %fusion.115 = bf16[1,512,4,64]{1,3,2,0:T(8,128)(2,1)S(1)} fusion(bf16[1024,4,64]{0,2,1:T(8,128)(2,1)S(1)} %bitcast.166, f32[4,512,1024]{2,1,0:T(8,128)} %fusion.141, f32[4,512,1024]{2,1,0:T(8,128)} %copy-done.5, f32[4,512]{1,0:T(4,128)S(1)} %log_add_fusion.1, pred[512,1024]{1,0:T(8,128)(4,1)} %copy-done.11), kind=kOutput, calls=%fused_computation.99 | convolution fusion | flops 291638272 | bytes 18096128 | tf_op jit(solution)/shard_map/bhqk,bkhd->bqhd/dot_general | solution.py:100
  290.1 23.5 %fusion.14 = f32[4,64,1024]{2,1,0:T(8,128)} fusion(f32[4,512,1024]{2,1,0:T(8,128)} %fusion.141, f32[4,512,1024]{2,1,0:T(8,128)} %copy-done.5, f32[4,512]{1,0:T(4,128)S(1)} %log_add_fusion.1, pred[512,1024]{1,0:T(8,128)(4,1)} %copy-done.11, bf16[1,1024,4,64]{1,3,2,0:T(8,128)(2,1)S(1)} %bitcast.163), kind=kOutput, calls=%fused_computation.23 | convolution fusion | flops 291507200 | bytes 35930112 | tf_op jit(solution)/shard_map/bhqk,bqhd->bkhd/dot_general | solution.py:104
  313.6 5.8 %fusion.59 = f32[4,64,1024]{2,1,0:T(8,128)} fusion(f32[4,512,1024]{2,1,0:T(8,128)} %copy-done.4, f32[4,512]{1,0:T(4,128)S(1)} %log_add_fusion, pred[512,1024]{1,0:T(8,128)(4,1)S(1)} %copy-done.10, bf16[1,1024,4,64]{1,3,2,0:T(8,128)(2,1)S(1)} %bitcast.171), kind=kOutput, calls=%fused_computation.53 | convolution fusion | flops 276824064 | bytes 10231808 | tf_op jit(solution)/shard_map/bhqk,bqhd->bkhd/dot_general | solution.py:107
  319.4 17.9 %fusion.118 = bf16[1,512,4,64]{1,3,2,0:T(8,128)(2,1)} fusion(bf16[1024,4,64]{0,2,1:T(8,128)(2,1)S(1)} %bitcast.167, f32[4,512,1024]{2,1,0:T(8,128)} %fusion.142, f32[4,512,1024]{2,1,0:T(8,128)} %copy-done.4, f32[4,512]{1,0:T(4,128)S(1)} %log_add_fusion, pred[512,1024]{1,0:T(8,128)(4,1)S(1)} %copy-done.10), kind=kOutput, calls=%fused_computation.100 | convolution fusion | flops 291638272 | bytes 18096128 | tf_op jit(solution)/shard_map/bhqk,bkhd->bqhd/dot_general | solution.py:100
  340.3 5.0 fusion.99
  348.7 22.9 %fusion.102 = bf16[4,64,1024]{2,1,0:T(8,128)(2,1)S(1)} fusion(f32[4,64,1024]{2,1,0:T(8,128)} %fusion.14, f32[4,512,1024]{2,1,0:T(8,128)} %fusion.142, f32[4,512,1024]{2,1,0:T(8,128)} %copy-done.4, f32[4,512]{1,0:T(4,128)S(1)} %log_add_fusion, pred[512,1024]{1,0:T(8,128)(4,1)} %copy-done.9, bf16[1,1024,4,64]{1,3,2,0:T(8,128)(2,1)} %bitcast.162), kind=kOutput, calls=%fused_computation.88 | convolution fusion | flops 292031488 | bytes 36454400 | tf_op jit(solution)/shard_map/bhqk,bqhd->bkhd/dot_general | solution.py:104
  372.6 3.7 fusion.145
  377.4 3.7 fusion.144
  382.1 7.6 %fusion.34 = bf16[1024,1024]{1,0:T(8,128)(2,1)} fusion(f32[1024,1024]{1,0:T(8,128)} %fusion.144, f32[1024,1024]{1,0:T(8,128)} %fusion.145, bf16[3,1024,256]{2,1,0:T(8,128)(2,1)} %param.12, bf16[1,1024,256]{2,1,0:T(8,128)(2,1)} %copy.19, bf16[1,1024,256]{2,1,0:T(8,128)(2,1)} %copy.18, bf16[1,1024,256]{2,1,0:T(8,128)(2,1)S(1)} %copy-done.23), kind=kOutput, calls=%fused_computation.37 | convolution fusion | flops 1615331328 | bytes 13631488 | tf_op jit(solution)/shard_map/stc,sdc->td/dot_general | solution.py:225
  389.8 78.4 %all-reduce.2.cloned.1.call-done = f32[4,4,1024]{2,1,0:T(4,128)} async-done(((f32[4,4,1024]{2,1,0:T(4,128)}), f32[4,4,1024]{2,1,0:T(4,128)}) %all-reduce.2.cloned.1.call-update) | async-done | bytes 65552 | tf_op jit(solution)/shard_map/psum | solution.py:274
  472.0 33.6 %reduce-scatter.11.cloned.1.call-done = bf16[256,1024]{1,0:T(8,128)(2,1)} async-done(((bf16[1024,1024]{1,0:T(8,128)(2,1)}), bf16[256,1024]{1,0:T(8,128)(2,1)}) %reduce-scatter.11.cloned.1.call-update) | async-done | bytes 524304 | tf_op jit(solution)/shard_map/reduce_scatter | solution.py:242
  507.4 2.7 multiply_add_fusion
  (127 shorter events, 34.7 us)
Async XLA Ops:
  7.2 122.0 %copy-start = (bf16[1024,1024]{1,0:T(8,128)(2,1)S(1)}, bf16[1024,1024]{1,0:T(8,128)(2,1)}, u32[]{:S(2)}) copy-start(bf16[1024,1024]{1,0:T(8,128)(2,1)} %param.14) | copy-start | bytes 6291460
  7.2 5.3 %copy-start.26 = (f32[4,4,1024]{2,1,0:T(4,128)S(1)}, f32[4,4,1024]{2,1,0:T(4,128)}, u32[]{:S(2)}) copy-start(f32[4,4,1024]{2,1,0:T(4,128)} %param.16) | copy-start | bytes 196612
  7.2 83.6 %reduce-scatter.5.cloned.1.call-start = ((), (), s32[]{:S(2)}) async-start(), calls=%async_computation.4 | async-start | bytes 2621440 | tf_op jit(solution)/shard_map/reduce_scatter | solution.py:189
  7.2 5.3 %copy-start.6 = (bf16[1024,1024]{1,0:T(8,128)(2,1)S(1)}, bf16[1024,1024]{1,0:T(8,128)(2,1)}, u32[]{:S(2)}) copy-start(bf16[1024,1024]{1,0:T(8,128)(2,1)} %param.10) | copy-start | bytes 6291460
  12.6 3.6 copy-start.20
  15.5 4.8 copy-start.2
  19.6 23.2 %copy-start.11 = (pred[512,1024]{1,0:T(8,128)(4,1)}, pred[512,1024]{1,0:T(8,128)(4,1)S(1)}, u32[]{:S(2)}) copy-start(pred[512,1024]{1,0:T(8,128)(4,1)S(1)} %iota_compare_fusion.1) | copy-start | bytes 1572868
  22.4 25.8 %copy-start.9 = (pred[512,1024]{1,0:T(8,128)(4,1)}, pred[512,1024]{1,0:T(8,128)(4,1)S(1)}, u32[]{:S(2)}) copy-start(pred[512,1024]{1,0:T(8,128)(4,1)S(1)} %iota_compare_fusion) | copy-start | bytes 1572868
  27.2 15.7 %copy-start.5 = (f32[4,512,1024]{2,1,0:T(8,128)}, f32[4,512,1024]{2,1,0:T(8,128)S(1)}, u32[]{:S(2)}) copy-start(f32[4,512,1024]{2,1,0:T(8,128)S(1)} %get-tuple-element.31) | copy-start | bytes 25165828
  28.9 19.3 %copy-start.4 = (f32[4,512,1024]{2,1,0:T(8,128)}, f32[4,512,1024]{2,1,0:T(8,128)S(1)}, u32[]{:S(2)}) copy-start(f32[4,512,1024]{2,1,0:T(8,128)S(1)} %get-tuple-element.29) | copy-start | bytes 25165828
  28.9 13.6 %copy-start.14 = (f32[1024,256]{0,1:T(8,128)S(1)}, f32[1024,256]{0,1:T(8,128)}, u32[]{:S(2)}) copy-start(f32[1024,256]{0,1:T(8,128)} %fusion.134) | copy-start | bytes 3145732
  42.9 5.3 %copy-start.7 = (bf16[1024,256]{0,1:T(8,128)(2,1)}, bf16[1024,256]{0,1:T(8,128)(2,1)S(1)}, u32[]{:S(2)}) copy-start(bf16[1024,256]{0,1:T(8,128)(2,1)S(1)} %fusion.105) | copy-start | bytes 1572868
  53.3 75.8 %all-gather.3.cloned.1.call-start = ((), (), s32[]{:S(2)}) async-start(), calls=%async_computation.5 | async-start | bytes 2621440 | tf_op jit(solution)/shard_map/all_gather | solution.py:194
  93.7 86.0 %reduce-scatter.9.cloned.1.call-start = ((), (), s32[]{:S(2)}) async-start(), calls=%async_computation.7 | async-start | bytes 2621440 | tf_op jit(solution)/shard_map/reduce_scatter | solution.py:208
  144.4 73.4 %reduce-scatter.7.cloned.1.call-start = ((), (), s32[]{:S(2)}) async-start(), calls=%async_computation.6 | async-start | bytes 2621440 | tf_op jit(solution)/shard_map/reduce_scatter | solution.py:205
  151.3 105.2 %copy-start.25 = (bf16[256,1024]{1,0:T(8,128)(2,1)S(1)}, bf16[256,1024]{1,0:T(8,128)(2,1)}, u32[]{:S(2)}) copy-start(bf16[256,1024]{1,0:T(8,128)(2,1)} %param.13) | copy-start | bytes 1572868
  151.3 105.2 %all-gather.5.cloned.1.call-start = ((), (), s32[]{:S(2)}) async-start(), calls=%async_computation.8 | async-start | bytes 2621440 | tf_op jit(solution)/shard_map/all_gather | solution.py:214
  221.0 37.8 %copy-start.8 = (bf16[1024,256]{0,1:T(8,128)(2,1)S(1)}, bf16[1024,256]{0,1:T(8,128)(2,1)}, u32[]{:S(2)}) copy-start(bf16[1024,256]{0,1:T(8,128)(2,1)} %copy-done.7) | copy-start | bytes 1572868
  221.0 247.2 %all-reduce.2.cloned.1.call-start = ((), (), s32[]{:S(2)}) async-start(), calls=%async_computation.10 | async-start | bytes 131072 | tf_op jit(solution)/shard_map/psum | solution.py:274
  221.1 69.0 %copy-start.29 = (f32[4,512]{1,0:T(4,128)}, f32[4,512]{1,0:T(4,128)S(1)}, u32[]{:S(2)}) copy-start(f32[4,512]{1,0:T(4,128)S(1)} %log_add_fusion.1) | copy-start | bytes 24580
  258.8 54.8 %copy-start.21 = (bf16[1024,256]{0,1:T(8,128)(2,1)}, bf16[1024,256]{0,1:T(8,128)(2,1)S(1)}, u32[]{:S(2)}) copy-start(bf16[1024,256]{0,1:T(8,128)(2,1)S(1)} %convolution_convert_fusion.1) | copy-start | bytes 1572868
  263.3 4.5 copy-start.18
  267.8 22.2 %copy-start.16 = (bf16[1024,256]{0,1:T(8,128)(2,1)S(1)}, bf16[1024,256]{0,1:T(8,128)(2,1)}, u32[]{:S(2)}) copy-start(bf16[1024,256]{0,1:T(8,128)(2,1)} %copy-done.15) | copy-start | bytes 1572868
  290.1 23.5 %copy-start.10 = (pred[512,1024]{1,0:T(8,128)(4,1)S(1)}, pred[512,1024]{1,0:T(8,128)(4,1)}, u32[]{:S(2)}) copy-start(pred[512,1024]{1,0:T(8,128)(4,1)} %copy-done.9) | copy-start | bytes 1572868
  319.3 19.1 %copy-start.3 = (bf16[1024,1024]{1,0:T(8,128)(2,1)S(1)}, bf16[1024,1024]{1,0:T(8,128)(2,1)}, u32[]{:S(2)}) copy-start(bf16[1024,1024]{1,0:T(8,128)(2,1)} %copy-done.2) | copy-start | bytes 6291460
  348.6 24.0 %copy-start.19 = (f32[1024,4]{1,0:T(8,128)S(1)}, f32[1024,4]{1,0:T(8,128)}, u32[]{:S(2)}) copy-start(f32[1024,4]{1,0:T(8,128)} %convolution_multiply_fusion.3) | copy-start | bytes 49156
  348.6 157.1 %reduce-scatter.11.cloned.1.call-start = ((), (), s32[]{:S(2)}) async-start(), calls=%async_computation.9 | async-start | bytes 2621440 | tf_op jit(solution)/shard_map/reduce_scatter | solution.py:242
  377.3 4.8 copy-start.23
  382.1 88.3 %copy-start.27 = (f32[4,4,1024]{2,1,0:T(4,128)S(1)}, f32[4,4,1024]{2,1,0:T(4,128)}, u32[]{:S(2)}) copy-start(f32[4,4,1024]{2,1,0:T(4,128)} %param.17) | copy-start | bytes 196612
  382.1 88.3 %copy-start.28 = (f32[4,4,1024]{2,1,0:T(4,128)S(1)}, f32[4,4,1024]{2,1,0:T(4,128)}, u32[]{:S(2)}) copy-start(f32[4,4,1024]{2,1,0:T(4,128)} %param.18) | copy-start | bytes 196612
  382.1 127.9 %copy-start.1 = (bf16[1024,1024]{1,0:T(8,128)(2,1)S(1)}, bf16[1024,1024]{1,0:T(8,128)(2,1)}, u32[]{:S(2)}) copy-start(bf16[1024,1024]{1,0:T(8,128)(2,1)} %param.14) | copy-start | bytes 6291460
  389.7 117.7 %copy-start.13 = (f32[256,1024]{1,0:T(8,128)S(1)}, f32[256,1024]{1,0:T(8,128)}, u32[]{:S(2)}) copy-start(f32[256,1024]{1,0:T(8,128)} %get-tuple-element.16) | copy-start | bytes 3145732
  (7 other events, 21.1 us)
Sparse Core Ops, SparseCore 0:
  53.4 37.2 reduce-scatter.4
  93.8 35.2 all-gather.2
  144.5 35.1 reduce-scatter.8
  182.5 35.1 reduce-scatter.6
  221.1 35.2 all-gather.4
  348.7 119.4 all-reduce.1
  471.4 34.2 reduce-scatter.10
where the time goes:
time: 520 us; the launch traced here: 518 us
  waiting for transfers between devices  281 us (54%)
  matrix products  171 us (33%)
  other arithmetic  44.5 us (9%)
  between operations  16.7 us (3%)
    psum x1, waiting for transfers between devices, body(): reduced = lax.psum(partial_grad, ('dp', 'tensor'))  78.4 us
    dot_general x2, matrix products, attention_backward(): jnp.einsum('bhqk,bqhd->bkhd', dscore, query_block, preferred_element_type...  46.4 us
    dot_general x2, matrix products, attention_backward(): jnp.einsum('bhqk,bkhd->bqhd', dscore, key_all, preferred_element_type=jnp...  40.1 us
    reduce_scatter x1, waiting for transfers between devices, body(): lax.psum_scatter(mlp_part.astype(jnp.bfloat16), 'tensor', scatter_dimensi...  36.7 us
    all_gather x1, waiting for transfers between devices, body(): lax.all_gather(normed_two_rows.astype(jnp.bfloat16), 'tensor', axis=0, ti...  35.4 us
    all_gather x1, waiting for transfers between devices, body(): lax.all_gather(resid_grad_rows.astype(jnp.bfloat16), 'tensor', axis=0, ti...  35.4 us
    reduce_scatter x1, waiting for transfers between devices, body(): lax.psum_scatter(first_part.astype(jnp.bfloat16), 'tensor', scatter_dimen...  33.6 us
    reduce_scatter x1, waiting for transfers between devices, body(): lax.psum_scatter(attn_part.astype(jnp.bfloat16), 'tensor', scatter_dimens...  33.4 us
  transfers between devices with their start and end apart: 7, of which 7 were waited for; matrix products, arithmetic and copies ran while one was open for 11% of the time, Pallas kernels for 0%

commit v1 on v0

--- a/solution.py
+++ b/solution.py
@@ -1,6 +1,10 @@
+import functools
+
 import jax
 import jax.numpy as jnp
 from jax import lax
+from jax.experimental import pallas as pl
+from jax.experimental.pallas import tpu as pltpu
 from jax.sharding import PartitionSpec as P
 
 HD = 64
@@ -17,6 +21,8 @@
 WEIGHT_DECAY = 0.01
 ADAM_EPSILON = 1e-08
 NEG_LARGE = -1e30
+GELU_SCALE = 0.7978845608028654
+GELU_CUBE = 0.044715
 
 
 def matrix_product(left, right):
@@ -287,6 +293,548 @@
     )
 
 
+MESH = pl.DeviceIdType.MESH
+BF = jnp.bfloat16
+F32 = jnp.float32
+GROUPS = 24
+ATTN_GROUPS = 8
+
+
+def mm(left, right):
+    return jnp.dot(left, right, preferred_element_type=F32)
+
+
+def mm_nt(left, right):
+    return lax.dot_general(left, right, (((1,), (1,)), ((), ())), preferred_element_type=F32)
+
+
+def mm_tn(left, right):
+    return lax.dot_general(left, right, (((0,), (0,)), ((), ())), preferred_element_type=F32)
+
+
+def flip(value, bit):
+    return value + bit - 2 * bit * ((value // bit) % 2)
+
+
+def unit_of(rows):
+    centered = rows - jnp.mean(rows, -1, keepdims=True)
+    inverse = lax.rsqrt(jnp.mean(centered * centered, -1, keepdims=True) + EPSILON)
+    return centered * inverse, inverse
+
+
+def fused_kernel(
+    planes,
+    tokens, norm_params, wqkv, w_out, w_fc, w_proj, factors, first_moment, second_moment, grad_out,
+    block_out, input_grad, clipped, grad_norm, factors_new, first_new, second_new,
+    tok, n1, go, wa, wo, fcw, pw, k_all, v_all, qs, p0, p1, p2, p3, mix, attn, attn_s, attn_r,
+    res, n2, mlp_acc, gnt_acc, mlp_s, mlp_r, gnt_s, gnt_r, gr_b, bo_s, bo_r, grf,
+    dk_acc, dv_acc, gq_scr, dos, gno_scr, gno_s, gno_r, chip_s, fin_r, tokr,
+    fpad, f02, f1p, f3p, down, gd_scr, fg_a, fg_b, ps, ps_r, plane_buf, z_buf, fin,
+    chain_send, chain_recv, load_sem, ssem, rsem,
+):
+    d = lax.axis_index("dp")
+    t = lax.axis_index("tensor")
+    z, c, x, y = d // 2, d % 2, t % 2, t // 2
+    odd = z % 2
+    nbr = (flip(d, 1), t)
+    prim = (d, flip(t, 1 + odd))
+    sec = (d, flip(t, 2 - odd))
+    zn = (flip(d, 2), t)
+    plane = [(d, flip(t, 1)), (d, flip(t, 2)), (d, 3 - t)]
+    zs = [(2 * ((z + k) % planes) + c, t) for k in range(1, planes)]
+    cross = [(flip(d, 1), flip(t, 2)), (flip(d, 1), 3 - t)]
+    dests = [(2 * z + y, 2 * c + j) for j in range(2)]
+    same = [jnp.logical_and(c == y, x == j) for j in range(2)]
+    quarter = [t, flip(t, 1 + odd), flip(t, 2 - odd), 3 - t]
+    column = [pl.multiple_of(q * 256 + c * 128, 128) for q in quarter]
+    block = [2 * i + (i + x) % 2 for i in range(4)]
+    block_row = [pl.multiple_of(b * 128, 128) for b in block]
+    own = pl.multiple_of(c * 256, 256)
+    other = pl.multiple_of(256 - c * 256, 256)
+    p_refs = (p0, p1, p2, p3)
+
+    def remote(src, dst, send, recv, device):
+        return pltpu.make_async_remote_copy(
+            src_ref=src, dst_ref=dst, send_sem=send, recv_sem=recv, device_id=device, device_id_type=MESH
+        )
+
+    def to_nbr(src, dst, index):
+        return remote(src, dst, ssem.at[index], rsem.at[index], nbr)
+
+    lane = pl.ds(pl.multiple_of(c * 128, 128), 128)
+    loads = [
+        pltpu.make_async_copy(wqkv.at[m, :, lane], wa.at[m, :, pl.ds(0, 128)], load_sem.at[m])
+        for m in range(3)
+    ]
+    loads.append(pltpu.make_async_copy(w_out.at[lane, :], wo.at[pl.ds(0, 128), :], load_sem.at[3]))
+    for h in range(2):
+        hidden = pl.ds(pl.multiple_of(c * 512 + h * 256, 256), 256)
+        loads.append(pltpu.make_async_copy(w_fc.at[:, hidden], fcw.at[0, h], load_sem.at[4 + 2 * h]))
+        loads.append(pltpu.make_async_copy(w_proj.at[hidden, :], pw.at[0, h], load_sem.at[5 + 2 * h]))
+    for load in loads:
+        load.start()
+    own_rows = pltpu.make_async_copy(
+        tokens.at[pl.ds(pl.multiple_of(t * 256, 256), 256), :], tokr, load_sem.at[8]
+    )
+    own_rows.start()
+
+    barrier = pltpu.get_barrier_semaphore()
+    partners = [nbr] + plane + zs + cross
+    for device in partners:
+        pl.semaphore_signal(barrier, inc=1, device_id=device, device_id_type=MESH)
+    pl.semaphore_wait(barrier, len(partners))
+
+    doc = [
+        (tokens.at[pl.ds(256 * r, 256), :], tok.at[pl.ds(256 * r, 256), :], r) for r in range(4)
+    ] + [
+        (grad_out.at[pl.ds(block_row[i], 128), :], go.at[pl.ds(128 * i, 128), :], 4 + i) for i in range(4)
+    ]
+
+    @pl.when(c == y)
+    def _():
+        for src, dst, index in doc:
+            to_nbr(src, dst, index).start()
+            pltpu.make_async_copy(src, dst, rsem.at[index]).start()
+
+    def doc_wait(index):
+        to_nbr(*doc[index]).wait_recv()
+
+    def piece(slot, group):
+        if group < ATTN_GROUPS:
+            m, a = group // 2, group % 2
+            if m < 3:
+                return wa.at[m, pl.ds(512 * a, 512), pl.ds(128 * slot, 128)]
+            return wo.at[pl.ds(128 * slot + 64 * a, 64), :]
+        h, r = (group - ATTN_GROUPS) // 8, (group - ATTN_GROUPS) % 8
+        if r < 4:
+            return fcw.at[slot, h, pl.ds(256 * r, 256), :]
+        return pw.at[slot, h, pl.ds(64 * (r - 4), 64), :]
+
+    def hop(slot, group):
+        return remote(
+            piece(1 if slot > 1 else 0, group),
+            piece(slot, group),
+            chain_send.at[slot - 1, group],
+            chain_recv.at[slot - 1, group],
+            (prim, zn, sec)[slot - 1],
+        )
+
+    for load in loads:
+        load.wait()
+    for group in range(GROUPS):
+        hop(1, group).start()
+
+    def pump(group):
+        hop(1, group).wait_recv()
+        hop(2, group).start()
+        hop(3, group).start()
+
+    fpad[...] = jnp.zeros_like(fpad)
+    fpad[0:4, :] = factors[0]
+    fpad[4:8, :] = factors[2]
+    f02[...] = fpad[...].astype(BF)
+    fpad[...] = jnp.zeros_like(fpad)
+    for s in range(4):
+        fpad[0:4, 128 * s : 128 * s + 128] = factors[1, :, pl.ds(column[s], 128)]
+        fpad[4:8, 512 + 128 * s : 640 + 128 * s] = factors[3, :, pl.ds(column[s], 128)]
+    f1p[...] = fpad[:, :512].astype(BF)
+    f3p[...] = fpad[:, 512:].astype(BF)
+    attn[...] = jnp.zeros_like(attn)
+    mlp_acc[...] = jnp.zeros_like(mlp_acc)
+    gnt_acc[...] = jnp.zeros_like(gnt_acc)
+    dk_acc[...] = jnp.zeros_like(dk_acc)
+    dv_acc[...] = jnp.zeros_like(dv_acc)
+    fg_a[...] = jnp.zeros_like(fg_a)
+    fg_b[...] = jnp.zeros_like(fg_b)
+    ps[...] = jnp.zeros_like(ps)
+
+    gain_one, bias_one = norm_params[0:1, :], norm_params[1:2, :]
+    gain_two, bias_two = norm_params[2:3, :], norm_params[3:4, :]
+    for r in range(4):
+        doc_wait(r)
+
+    @pl.loop(0, 8)
+    def _(r):
+        rows = pl.ds(pl.multiple_of(r * 128, 128), 128)
+        unit, _ = unit_of(tok[rows, :].astype(F32))
+        n1[rows, :] = (unit * gain_one + bias_one).astype(BF)
+
+    @pl.loop(0, 4)
+    def _(r):
+        rows = pl.ds(pl.multiple_of(r * 256, 256), 256)
+        down[rows, :] = mm_nt(n1[rows, :], f02[...]).astype(BF)
+
+    for group in range(ATTN_GROUPS):
+        pump(group)
+    for group in range(ATTN_GROUPS):
+        hop(2, group).wait_recv()
+        hop(3, group).wait_recv()
+    pump(8)
+
+    first_head = lax.broadcasted_iota(jnp.int32, (128, 512), 1) % 128 < 64
+
+    def stacked(rows):
+        return jnp.concatenate(
+            (jnp.where(first_head, rows, 0.0), jnp.where(first_head, 0.0, rows)), 0
+        ).astype(BF)
+
+    for i in range(4):
+        rows = pl.ds(block_row[i], 128)
+        query = mm(n1[rows, :], wa[0]) + ADAPTER_SCALING * mm(down[rows, :], f1p[...])
+        qs[i] = stacked(query.astype(BF).astype(F32) * 0.125)
+    pump(9)
+
+    @pl.loop(0, 4)
+    def _(r):
+        rows = pl.ds(pl.multiple_of(r * 256, 256), 256)
+        k_all[rows, :] = mm(n1[rows, :], wa[1]).astype(BF)
+
+    pump(10)
+
+    @pl.loop(0, 4)
+    def _(r):
+        rows = pl.ds(pl.multiple_of(r * 256, 256), 256)
+        v_all[rows, :] = (
+            mm(n1[rows, :], wa[2]) + ADAPTER_SCALING * mm(down[rows, :], f3p[...])
+        ).astype(BF)
+
+    pump(11)
+
+    def forward(i):
+        keys = 256 * (i + 1)
+        query_pos = lax.broadcasted_iota(jnp.int32, (256, keys), 0) % 128 + block[i] * 128
+        allowed = lax.broadcasted_iota(jnp.int32, (256, keys), 1) <= query_pos
+
+        @pl.loop(0, 4)
+        def _(s):
+            lanes = pl.ds(pl.multiple_of(s * 128, 128), 128)
+            scores = mm_nt(qs[i, :, lanes], k_all[0:keys, lanes])
+            scores = jnp.where(allowed, scores, NEG_LARGE)
+            exponent = jnp.exp(scores - jnp.max(scores, -1, keepdims=True))
+            probability = (exponent / jnp.sum(exponent, -1, keepdims=True)).astype(BF)
+            p_refs[i][s] = probability
+            both = mm(probability, v_all[0:keys, lanes])
+            mix[128 * i : 128 * i + 128, lanes] = jnp.where(
+                first_head[:, 0:128], both[0:128], both[128:256]
+            ).astype(BF)
+
+    forward(0)
+    forward(1)
+    pump(12)
+    forward(2)
+    pump(13)
+    forward(3)
+    pump(14)
+
+    @pl.loop(0, 2)
+    def _(r):
+        rows = pl.ds(pl.multiple_of(r * 256, 256), 256)
+        attn[rows, :] = mm(mix[rows, :], wo[...])
+
+    attn_s[...] = attn[pl.ds(other, 256), :].astype(BF)
+    to_nbr(attn_s, attn_r, 8).start()
+    pump(15)
+    to_nbr(attn_s, attn_r, 8).wait_recv()
+    for j in range(2):
+        part = slice(128 * j, 128 * j + 128)
+        start = pl.multiple_of(128 * (4 * c + 2 * j + (j + x) % 2), 128)
+        rows = (
+            tok[pl.ds(start, 128), :].astype(F32)
+            + attn[pl.ds(pl.multiple_of(own + 128 * j, 128), 128), :]
+            + attn_r[part, :].astype(F32)
+        )
+        res[part, :] = rows
+        unit, _ = unit_of(rows)
+        n2[pl.ds(pl.multiple_of(own + 128 * j, 128), 128), :] = (unit * gain_two + bias_two).astype(BF)
+    half = pl.ds(own, 256)
+    to_nbr(n2.at[half, :], n2.at[half, :], 9).start()
+    for i in range(4):
+        doc_wait(4 + i)
+
+    def feed_forward(slot, h):
+        @pl.loop(0, 2)
+        def _(r):
+            rows = pl.ds(pl.multiple_of(r * 256, 256), 256)
+            pre = mm(n2[rows, :], fcw[slot, h])
+            square = pre * pre
+            tanh = jnp.tanh(GELU_SCALE * pre * (1.0 + GELU_CUBE * square))
+            half_up = 0.5 * (1.0 + tanh)
+            slope = half_up + (0.5 * GELU_SCALE) * pre * (1.0 - tanh * tanh) * (
+                1.0 + 3.0 * GELU_CUBE * square
+            )
+            mlp_acc[rows, :] += mm((pre * half_up).astype(BF), pw[slot, h])
+            grad_pre = (mm_nt(go[rows, :], pw[slot, h]) * slope).astype(BF)
+            gnt_acc[rows, :] += mm_nt(grad_pre, fcw[slot, h])
+
+    rest = pl.ds(other, 256)
+    to_nbr(n2.at[rest, :], n2.at[rest, :], 9).wait_recv()
+    feed_forward(0, 0)
+    pump(16)
+    feed_forward(0, 1)
+    pump(17)
+    feed_forward(1, 0)
+    pump(18)
+    for slot in (2, 3):
+        for group in range(8, 16):
+            hop(slot, group).wait_recv()
+        feed_forward(slot, 0)
+        pump(17 + slot)
+    for group in range(21, GROUPS):
+        pump(group)
+    feed_forward(1, 1)
+    for slot in (2, 3):
+        for group in range(16, GROUPS):
+            hop(slot, group).wait_recv()
+        feed_forward(slot, 1)
+
+    gnt_s[...] = gnt_acc[rest, :].astype(BF)
+    to_nbr(gnt_s, gnt_r, 11).start()
+    mlp_s[...] = mlp_acc[rest, :].astype(BF)
+    to_nbr(mlp_s, mlp_r, 10).start()
+    to_nbr(gnt_s, gnt_r, 11).wait_recv()
+    for j in range(2):
+        part = slice(128 * j, 128 * j + 128)
+        mine = pl.ds(pl.multiple_of(own + 128 * j, 128), 128)
+        unit, inverse = unit_of(res[part, :])
+        scaled = (gnt_acc[mine, :] + gnt_r[part, :].astype(F32)) * gain_two
+        grad = go[mine, :].astype(F32) + inverse * (
+            scaled
+            - jnp.mean(scaled, -1, keepdims=True)
+            - unit * jnp.mean(scaled * unit, -1, keepdims=True)
+        )
+        gr_b[mine, :] = grad.astype(BF)
+    to_nbr(gr_b.at[half, :], gr_b.at[half, :], 12).start()
+
+    def to_owner(src, dst, j, first):
+        send, recv = ssem.at[first + j], rsem.at[first + x]
+
+        @pl.when(same[j])
+        def _():
+            pltpu.make_async_copy(src, dst, recv).start()
+
+        @pl.when(jnp.logical_not(same[j]))
+        def _():
+            remote(src, dst, send, recv, dests[j]).start()
+
+    def owner_sent(src, dst, j, first):
+        @pl.when(jnp.logical_not(same[j]))
+        def _():
+            remote(src, dst, ssem.at[first + j], rsem.at[first + x], dests[j]).wait_send()
+
+    to_nbr(mlp_s, mlp_r, 10).wait_recv()
+    for j in range(2):
+        part = slice(128 * j, 128 * j + 128)
+        mine = pl.ds(pl.multiple_of(own + 128 * j, 128), 128)
+        bo_s[part, :] = (res[part, :] + mlp_acc[mine, :] + mlp_r[part, :].astype(F32)).astype(BF)
+    late = []
+    for j in range(2):
+        place = pl.ds(pl.multiple_of(128 * ((j + x) % 2), 128), 128)
+        mine = pl.ds(pl.multiple_of(own + 128 * j, 128), 128)
+        late.append((gr_b.at[mine, :], grf.at[place, :], j, 20))
+        late.append((bo_s.at[pl.ds(128 * j, 128), :], bo_r.at[place, :], j, 22))
+    for item in late:
+        to_owner(*item)
+    to_nbr(gr_b.at[rest, :], gr_b.at[rest, :], 12).wait_recv()
+
+    for i in range(4):
+        grad_mixture = mm_nt(gr_b[128 * i : 128 * i + 128, :], wo[...])
+        dos[i] = stacked(grad_mixture.astype(BF).astype(F32))
+
+    def backward(i):
+        keys = 256 * (i + 1)
+
+        @pl.loop(0, 4)
+        def _(s):
+            lanes = pl.ds(pl.multiple_of(s * 128, 128), 128)
+            prob_low = p_refs[i][s]
+            probability = prob_low.astype(F32)
+            grad_rows = dos[i, :, lanes]
+            grad_prob = mm_nt(grad_rows, v_all[0:keys, lanes])
+            delta = jnp.sum(grad_prob * probability, -1, keepdims=True)
+            dscore = (probability * (grad_prob - delta)).astype(BF)
+            both = 0.125 * mm(dscore, k_all[0:keys, lanes])
+            gq_scr[:, lanes] = jnp.where(first_head[:, 0:128], both[0:128], both[128:256]).astype(BF)
+            dk_acc[0:keys, lanes] += mm_tn(dscore, qs[i, :, lanes])
+            dv_acc[0:keys, lanes] += mm_tn(prob_low, grad_rows)
+
+        rows = slice(256 * i, 256 * i + 256)
+        place = pl.ds(pl.multiple_of(128 * ((i + x) % 2), 128), 128)
+        grad_query = gq_scr[...]
+        grad_keys = dk_acc[rows, :].astype(BF)
+        grad_values = dv_acc[rows, :].astype(BF)
+        gd_scr[...] = ADAPTER_SCALING * mm_nt(grad_values, f3p[...])
+        gd_scr[place, :] += ADAPTER_SCALING * mm_nt(grad_query, f1p[...])
+        grad_down = gd_scr[...].astype(BF)
+        gno_scr[...] = mm_nt(grad_keys, wa[1]) + mm_nt(grad_values, wa[2]) + mm(grad_down, f02[...])
+        gno_scr[place, :] += mm_nt(grad_query, wa[0])
+        gno_s[i] = gno_scr[...].astype(BF)
+
+        @pl.when(c != i // 2)
+        def _():
+            to_nbr(gno_s.at[i], gno_r.at[i % 2], 13 + i).start()
+
+        fg_a[...] += mm_tn(grad_down, n1[rows, :])[0:8]
+        up_query = mm_tn(down[pl.ds(block_row[i], 128), :], grad_query)[0:8]
+        up_value = mm_tn(down[rows, :], grad_values)[0:8]
+        upper = lax.broadcasted_iota(jnp.int32, (8, 512), 0) < 4
+        fg_b[...] += ADAPTER_SCALING * jnp.where(upper, up_query, up_value)
+
+    def reduce_rows(i):
+        @pl.when(c == i // 2)
+        def _():
+            to_nbr(gno_s.at[i], gno_r.at[i % 2], 13 + i).wait_recv()
+            chip_s[i % 2] = (gno_s[i].astype(F32) + gno_r[i % 2].astype(F32)).astype(BF)
+            to_owner(chip_s.at[i % 2], fin_r.at[x], i % 2, 24)
+
+    backward(3)
+    backward(2)
+    reduce_rows(3)
+    backward(1)
+    reduce_rows(2)
+    backward(0)
+    reduce_rows(1)
+
+    ps[0:8, :] = fg_a[...]
+    for s in range(4):
+        ps[8:16, pl.ds(column[s], 128)] = fg_b[:, 128 * s : 128 * s + 128]
+    to_nbr(ps, ps_r, 17).start()
+    reduce_rows(0)
+    to_nbr(ps, ps_r, 17).wait_recv()
+    mine = pl.ds(pl.multiple_of(8 * c, 8), 8)
+    plane_buf[t] = ps[mine, :] + ps_r[mine, :]
+    copies = []
+    for k, device in enumerate(plane):
+        copies.append(remote(plane_buf.at[t], plane_buf.at[t], ssem.at[28 + k], rsem.at[28 + k], device))
+        copies[-1].start()
+    for copy in copies:
+        copy.wait_recv()
+    z_buf[z] = plane_buf[0] + plane_buf[1] + plane_buf[2] + plane_buf[3]
+    z_copies = []
+    for k, device in enumerate(zs):
+        z_copies.append(remote(z_buf.at[z], z_buf.at[z], ssem.at[31 + k], rsem.at[31 + k], device))
+        z_copies[-1].start()
+
+    own_rows.wait()
+    for first in (20, 22):
+        for sender in range(2):
+            place = pl.ds(128 * sender, 128)
+            remote(bo_s.at[pl.ds(0, 128), :], bo_r.at[place, :], ssem.at[first], rsem.at[first + sender], dests[0]).wait_recv()
+    block_out[...] = bo_r[...]
+    for sender in range(2):
+        remote(chip_s.at[0], fin_r.at[sender], ssem.at[24], rsem.at[24 + sender], dests[0]).wait_recv()
+
+    @pl.loop(0, 2)
+    def _(r):
+        rows = pl.ds(pl.multiple_of(r * 128, 128), 128)
+        unit, inverse = unit_of(tokr[rows, :].astype(F32))
+        scaled = (fin_r[0, rows, :].astype(F32) + fin_r[1, rows, :].astype(F32)) * gain_one
+        input_grad[rows, :] = grf[rows, :].astype(F32) + inverse * (
+            scaled
+            - jnp.mean(scaled, -1, keepdims=True)
+            - unit * jnp.mean(scaled * unit, -1, keepdims=True)
+        )
+
+    for copy in z_copies:
+        copy.wait_recv()
+    total = z_buf[0]
+    for k in range(1, planes):
+        total = total + z_buf[k]
+    fin[mine, :] = total
+    to_nbr(fin.at[mine, :], fin.at[mine, :], 18).start()
+    theirs = pl.ds(pl.multiple_of(8 - 8 * c, 8), 8)
+    to_nbr(fin.at[theirs, :], fin.at[theirs, :], 18).wait_recv()
+
+    grad = fin[...]
+    norm = jnp.sqrt(jnp.sum(grad * grad, (0, 1), keepdims=True))
+    grad_norm[...] = norm
+    grad = grad * (CLIP_NORM / jnp.maximum(norm, CLIP_NORM))
+    for index, first in enumerate((0, 8, 4, 12)):
+        value, weights = grad[first : first + 4], factors[index]
+        first_value = BETA_ONE * first_moment[index] + (1.0 - BETA_ONE) * value
+        second_value = BETA_TWO * second_moment[index] + (1.0 - BETA_TWO) * value * value
+        first_hat = first_value / (1.0 - BETA_ONE**STEP)
+        second_hat = second_value / (1.0 - BETA_TWO**STEP)
+        clipped[index] = value
+        first_new[index] = first_value
+        second_new[index] = second_value
+        factors_new[index] = weights - LEARN_RATE * (
+            first_hat / (jnp.sqrt(second_hat) + ADAM_EPSILON) + WEIGHT_DECAY * weights
+        )
+
+    @pl.when(c == y)
+    def _():
+        for item in doc:
+            to_nbr(*item).wait_send()
+
+    for slot in (1, 2, 3):
+        for group in range(GROUPS):
+            hop(slot, group).wait_send()
+    to_nbr(attn_s, attn_r, 8).wait_send()
+    to_nbr(n2.at[half, :], n2.at[half, :], 9).wait_send()
+    to_nbr(mlp_s, mlp_r, 10).wait_send()
+    to_nbr(gnt_s, gnt_r, 11).wait_send()
+    to_nbr(gr_b.at[half, :], gr_b.at[half, :], 12).wait_send()
+    to_nbr(ps, ps_r, 17).wait_send()
+    to_nbr(fin.at[mine, :], fin.at[mine, :], 18).wait_send()
+    for item in late:
+        owner_sent(*item)
+    for i in range(4):
+
+        @pl.when(c != i // 2)
+        def _():
+            to_nbr(gno_s.at[i], gno_r.at[i % 2], 13 + i).wait_send()
+
+    for j in range(2):
+        owner_sent(chip_s.at[j], fin_r.at[x], j, 24)
+    for copy in copies + z_copies:
+        copy.wait_send()
+
+
+def fused(planes, *args):
+    vmem = pl.BlockSpec(memory_space=pltpu.VMEM)
+    hbm = pl.BlockSpec(memory_space=pl.ANY)
+
+    def buf(*shape, dtype=BF):
+        return pltpu.VMEM(shape, dtype)
+
+    def acc(*shape):
+        return pltpu.VMEM(shape, F32)
+
+    scratch = [
+        buf(1024, 1024), buf(1024, 1024), buf(512, 1024), buf(3, 1024, 512), buf(512, 1024),
+        buf(4, 2, 1024, 256), buf(4, 2, 256, 1024), buf(1024, 512), buf(1024, 512), buf(4, 256, 512),
+        buf(4, 256, 256), buf(4, 256, 512), buf(4, 256, 768), buf(4, 256, 1024), buf(512, 512),
+        acc(512, 1024), buf(256, 1024), buf(256, 1024),
+        acc(256, 1024), buf(512, 1024), acc(512, 1024), acc(512, 1024),
+        buf(256, 1024), buf(256, 1024), buf(256, 1024), buf(256, 1024), buf(512, 1024),
+        buf(256, 1024), buf(256, 1024), buf(256, 1024),
+        acc(1024, 512), acc(1024, 512), buf(128, 512), buf(4, 256, 512), acc(256, 1024),
+        buf(4, 256, 1024), buf(2, 256, 1024), buf(2, 256, 1024), buf(2, 256, 1024), buf(256, 1024),
+        acc(128, 1024), buf(128, 1024), buf(128, 512), buf(128, 512), buf(1024, 128), acc(256, 128),
+        acc(8, 1024), acc(8, 512), acc(16, 1024), acc(16, 1024), acc(4, 8, 1024), acc(planes, 8, 1024),
+        acc(16, 1024),
+        pltpu.SemaphoreType.DMA((3, GROUPS)), pltpu.SemaphoreType.DMA((3, GROUPS)),
+        pltpu.SemaphoreType.DMA((9,)), pltpu.SemaphoreType.DMA((31 + planes,)),
+        pltpu.SemaphoreType.DMA((31 + planes,)),
+    ]
+    small = jax.ShapeDtypeStruct((4, 4, 1024), F32)
+    outs = pl.pallas_call(
+        functools.partial(fused_kernel, planes),
+        name="block_step",
+        out_shape=(
+            jax.ShapeDtypeStruct((256, 1024), BF), jax.ShapeDtypeStruct((256, 1024), F32), small,
+            jax.ShapeDtypeStruct((1, 1), F32), small, small, small,
+        ),
+        in_specs=[hbm, vmem, hbm, hbm, hbm, hbm, vmem, vmem, vmem, hbm],
+        out_specs=(vmem,) * 7,
+        scratch_shapes=scratch,
+        compiler_params=pltpu.CompilerParams(
+            collective_id=1, has_side_effects=True, vmem_limit_bytes=62 << 20
+        ),
+    )(*args)
+    return outs[:3] + (outs[3].reshape(()),) + outs[4:]
+
+
 def solution(mesh):
     placed = (
         P("dp", None),
@@ -300,8 +848,18 @@
         P(),
         P("dp", None),
     )
+    planes = mesh.shape["dp"] // 2
+
+    def step(*args):
+        rows, width = args[0].shape
+        shapes = (rows, width, args[4].shape[1], args[2].shape[2], args[6].shape[1])
+        fits = mesh.shape["tensor"] == 4 and mesh.shape["dp"] % 4 == 0
+        if fits and shapes == (SEQ, 1024, 1024, 256, 4):
+            return fused(planes, *args)
+        return body(*args)
+
     return jax.shard_map(
-        body,
+        step,
         mesh=mesh,
         in_specs=placed,
         out_specs=(P(("dp", "tensor"), None), P(("dp", "tensor"), None), P(), P(), P(), P(), P()),

time: 520 us -> 146 us (0.28)
  waiting for transfers between devices: 281 us -> 0 us
  matrix products: 171 us -> 0 us
  Pallas kernels: 0 us -> 137 us
  other arithmetic: 44.5 us -> 0 us
  between operations: 16.7 us -> 2.37 us
    dot_general x35 -> x0, matrix products: 171 us -> none  [the longest x2 46.4 us: attention_backward(): jnp.einsum('bhqk,bqhd->bkhd', dscore, query_block, preferred_element_type...]
    pallas_call x0 -> x1, Pallas kernels: none -> 137 us  [fused(): pl.pallas_call(functools.partial(fused_kernel, planes), name='block_step'...]
    reduce_scatter x4 -> x0, waiting for transfers between devices: 132 us -> none  [the longest x1 36.7 us: body(): lax.psum_scatter(mlp_part.astype(jnp.bfloat16), 'tensor', scatter_dimensi...]
    psum x1 -> x0, waiting for transfers between devices: 78.4 us -> none  [body(): reduced = lax.psum(partial_grad, ('dp', 'tensor'))]
    all_gather x2 -> x0, waiting for transfers between devices: 70.8 us -> none  [the longest x1 35.4 us: body(): lax.all_gather(normed_two_rows.astype(jnp.bfloat16), 'tensor', axis=0, ti...]
    reduce_sum x9 -> x0, other arithmetic: 26.6 us -> none  [the longest x2 16 us: attention_forward(): row_total = jnp.sum(exponent, -1, keepdims=True)]
    convert_element_type x4 -> x0, other arithmetic: 8.24 us -> none  [the longest x1 3.98 us: body(): inputs = tokens_in.astype(jnp.float32)]
    unnamed x64 -> x14, local copies, waits for them, and re-layouts: 0.14 us -> 6.77 us
  transfers between devices with their start and end apart: 7 -> 0, of which waited for: 7 -> 0; matrix products, arithmetic and copies ran while one was open for 11% -> 0% of each run, Pallas kernels for 0% -> 0%
where the time goes in v1:
time: 146 us
  Pallas kernels  137 us (94%)
  local copies, waits for them, and re-layouts  6.77 us (5%)
  between operations  2.37 us (2%)
    pallas_call x1, Pallas kernels, fused(): pl.pallas_call(functools.partial(fused_kernel, planes), name='block_step'...  137 us
    unnamed x14, local copies, waits for them, and re-layouts  6.77 us

profile of v1, /device:TPU:1, one launch (start us, length us, event | category | flops | bytes accessed | tf_op | source)
XLA Modules:
  0.0 145.8 jit_solution(7105494623732509054)
XLA Ops:
  0.6 136.7 %block_step.1 = (bf16[256,1024]{1,0:T(8,128)(2,1)}, f32[256,1024]{1,0:T(8,128)}, f32[4,4,1024]{2,1,0:T(4,128)}, f32[1,1]{1,0:T(1,128)}, f32[4,4,1024]{2,1,0:T(4,...) custom-call(bf16[1024,1024]{1,0:T(8,128)(2,1)} %tokens.1, f32[4,1024]{1,0:T(4,128)} %norm_params.1, ...), custom_call_target="tpu_custom_call" | custom-call | tf_op jit(solution)/shard_map/block_step/pallas_call | solution.py:821
  137.3 0.0 copy-start.3
  137.3 0.0 copy-start.2
  137.4 0.0 copy-start.1
  137.4 0.0 copy-start
  137.4 1.9 %copy.24 = bf16[256,1024]{1,0:T(8,128)(2,1)} copy(bf16[256,1024]{1,0:T(8,128)(2,1)} %get-tuple-element.28) | data formatting | bytes 1048576
  139.3 2.3 %copy.25 = f32[256,1024]{1,0:T(8,128)} copy(f32[256,1024]{1,0:T(8,128)} %get-tuple-element.29) | data formatting | bytes 2097152
  141.6 0.0 copy-done.3
  141.6 0.6 copy.26
  142.8 0.0 copy-done.2
  142.8 0.6 copy.28
  143.4 0.0 copy-done.1
  143.4 0.6 copy.29
  144.1 0.0 copy-done
  144.1 0.6 copy.30
Async XLA Ops:
  137.3 4.3 %copy-start.3 = (f32[4,4,1024]{2,1,0:T(4,128)S(1)}, f32[4,4,1024]{2,1,0:T(4,128)}, u32[]{:S(2)}) copy-start(f32[4,4,1024]{2,1,0:T(4,128)} %get-tuple-element.30) | copy-start | bytes 196612
  137.3 5.4 %copy-start.2 = (f32[4,4,1024]{2,1,0:T(4,128)S(1)}, f32[4,4,1024]{2,1,0:T(4,128)}, u32[]{:S(2)}) copy-start(f32[4,4,1024]{2,1,0:T(4,128)} %get-tuple-element.32) | copy-start | bytes 196612
  137.4 6.1 %copy-start.1 = (f32[4,4,1024]{2,1,0:T(4,128)S(1)}, f32[4,4,1024]{2,1,0:T(4,128)}, u32[]{:S(2)}) copy-start(f32[4,4,1024]{2,1,0:T(4,128)} %get-tuple-element.33) | copy-start | bytes 196612
  137.4 6.7 %copy-start = (f32[4,4,1024]{2,1,0:T(4,128)S(1)}, f32[4,4,1024]{2,1,0:T(4,128)}, u32[]{:S(2)}) copy-start(f32[4,4,1024]{2,1,0:T(4,128)} %get-tuple-element.34) | copy-start | bytes 196612

commit v2 on v1

--- a/solution.py
+++ b/solution.py
@@ -324,11 +324,11 @@
 
 def fused_kernel(
     planes,
-    tokens, norm_params, wqkv, w_out, w_fc, w_proj, factors, first_moment, second_moment, grad_out,
-    block_out, input_grad, clipped, grad_norm, factors_new, first_new, second_new,
+    tokens, norm_params, wqkv, w_out, w_fc, w_proj, factors, grad_out,
+    bo_r, grf, fin_r, tokr, summed,
     tok, n1, go, wa, wo, fcw, pw, k_all, v_all, qs, p0, p1, p2, p3, mix, attn, attn_s, attn_r,
-    res, n2, mlp_acc, gnt_acc, mlp_s, mlp_r, gnt_s, gnt_r, gr_b, bo_s, bo_r, grf,
-    dk_acc, dv_acc, gq_scr, dos, gno_scr, gno_s, gno_r, chip_s, fin_r, tokr,
+    res, n2, mlp_acc, gnt_acc, mlp_s, mlp_r, gnt_s, gnt_r, gr_b, bo_s,
+    dk_acc, dv_acc, gq_scr, dos, gno_scr, gno_s, gno_r, chip_s,
     fpad, f02, f1p, f3p, down, gd_scr, fg_a, fg_b, ps, ps_r, plane_buf, z_buf, fin,
     chain_send, chain_recv, load_sem, ssem, rsem,
 ):
@@ -339,10 +339,8 @@
     nbr = (flip(d, 1), t)
     prim = (d, flip(t, 1 + odd))
     sec = (d, flip(t, 2 - odd))
-    zn = (flip(d, 2), t)
     plane = [(d, flip(t, 1)), (d, flip(t, 2)), (d, 3 - t)]
-    zs = [(2 * ((z + k) % planes) + c, t) for k in range(1, planes)]
-    cross = [(flip(d, 1), flip(t, 2)), (flip(d, 1), 3 - t)]
+    zs = [(flip(d, 2 << k), t) for k in range(planes.bit_length() - 1)]
     dests = [(2 * z + y, 2 * c + j) for j in range(2)]
     same = [jnp.logical_and(c == y, x == j) for j in range(2)]
     quarter = [t, flip(t, 1 + odd), flip(t, 2 - odd), 3 - t]
@@ -360,6 +358,16 @@
 
     def to_nbr(src, dst, index):
         return remote(src, dst, ssem.at[index], rsem.at[index], nbr)
+
+    pending = []
+
+    def drain():
+        for wait in pending:
+            wait()
+
+    def send(copy):
+        copy.start()
+        pending.append(copy.wait_send)
 
     lane = pl.ds(pl.multiple_of(c * 128, 128), 128)
     loads = [
@@ -379,7 +387,7 @@
     own_rows.start()
 
     barrier = pltpu.get_barrier_semaphore()
-    partners = [nbr] + plane + zs + cross
+    partners = [nbr] + plane[:2] + zs
     for device in partners:
         pl.semaphore_signal(barrier, inc=1, device_id=device, device_id_type=MESH)
     pl.semaphore_wait(barrier, len(partners))
@@ -395,6 +403,14 @@
         for src, dst, index in doc:
             to_nbr(src, dst, index).start()
             pltpu.make_async_copy(src, dst, rsem.at[index]).start()
+
+    def doc_sent():
+        @pl.when(c == y)
+        def _():
+            for item in doc:
+                to_nbr(*item).wait_send()
+
+    pending.append(doc_sent)
 
     def doc_wait(index):
         to_nbr(*doc[index]).wait_recv()
@@ -416,18 +432,18 @@
             piece(slot, group),
             chain_send.at[slot - 1, group],
             chain_recv.at[slot - 1, group],
-            (prim, zn, sec)[slot - 1],
+            (prim, zs[0], sec)[slot - 1],
         )
 
     for load in loads:
         load.wait()
     for group in range(GROUPS):
-        hop(1, group).start()
+        send(hop(1, group))
 
     def pump(group):
         hop(1, group).wait_recv()
-        hop(2, group).start()
-        hop(3, group).start()
+        send(hop(2, group))
+        send(hop(3, group))
 
     fpad[...] = jnp.zeros_like(fpad)
     fpad[0:4, :] = factors[0]
@@ -532,7 +548,7 @@
         attn[rows, :] = mm(mix[rows, :], wo[...])
 
     attn_s[...] = attn[pl.ds(other, 256), :].astype(BF)
-    to_nbr(attn_s, attn_r, 8).start()
+    send(to_nbr(attn_s, attn_r, 8))
     pump(15)
     to_nbr(attn_s, attn_r, 8).wait_recv()
     for j in range(2):
@@ -547,7 +563,7 @@
         unit, _ = unit_of(rows)
         n2[pl.ds(pl.multiple_of(own + 128 * j, 128), 128), :] = (unit * gain_two + bias_two).astype(BF)
     half = pl.ds(own, 256)
-    to_nbr(n2.at[half, :], n2.at[half, :], 9).start()
+    send(to_nbr(n2.at[half, :], n2.at[half, :], 9))
     for i in range(4):
         doc_wait(4 + i)
 
@@ -588,9 +604,9 @@
         feed_forward(slot, 1)
 
     gnt_s[...] = gnt_acc[rest, :].astype(BF)
-    to_nbr(gnt_s, gnt_r, 11).start()
+    send(to_nbr(gnt_s, gnt_r, 11))
     mlp_s[...] = mlp_acc[rest, :].astype(BF)
-    to_nbr(mlp_s, mlp_r, 10).start()
+    send(to_nbr(mlp_s, mlp_r, 10))
     to_nbr(gnt_s, gnt_r, 11).wait_recv()
     for j in range(2):
         part = slice(128 * j, 128 * j + 128)
@@ -603,10 +619,10 @@
             - unit * jnp.mean(scaled * unit, -1, keepdims=True)
         )
         gr_b[mine, :] = grad.astype(BF)
-    to_nbr(gr_b.at[half, :], gr_b.at[half, :], 12).start()
+    send(to_nbr(gr_b.at[half, :], gr_b.at[half, :], 12))
 
     def to_owner(src, dst, j, first):
-        send, recv = ssem.at[first + j], rsem.at[first + x]
+        recv = rsem.at[first + x]
 
         @pl.when(same[j])
         def _():
@@ -614,7 +630,7 @@
 
         @pl.when(jnp.logical_not(same[j]))
         def _():
-            remote(src, dst, send, recv, dests[j]).start()
+            remote(src, dst, ssem.at[first + j], recv, dests[j]).start()
 
     def owner_sent(src, dst, j, first):
         @pl.when(jnp.logical_not(same[j]))
@@ -634,13 +650,14 @@
         late.append((bo_s.at[pl.ds(128 * j, 128), :], bo_r.at[place, :], j, 22))
     for item in late:
         to_owner(*item)
+        pending.append(functools.partial(owner_sent, *item))
     to_nbr(gr_b.at[rest, :], gr_b.at[rest, :], 12).wait_recv()
 
     for i in range(4):
         grad_mixture = mm_nt(gr_b[128 * i : 128 * i + 128, :], wo[...])
         dos[i] = stacked(grad_mixture.astype(BF).astype(F32))
 
-    def backward(i):
+    def scores_back(i):
         keys = 256 * (i + 1)
 
         @pl.loop(0, 4)
@@ -657,27 +674,40 @@
             dk_acc[0:keys, lanes] += mm_tn(dscore, qs[i, :, lanes])
             dv_acc[0:keys, lanes] += mm_tn(prob_low, grad_rows)
 
+    def factors_back(i):
         rows = slice(256 * i, 256 * i + 256)
         place = pl.ds(pl.multiple_of(128 * ((i + x) % 2), 128), 128)
         grad_query = gq_scr[...]
-        grad_keys = dk_acc[rows, :].astype(BF)
         grad_values = dv_acc[rows, :].astype(BF)
         gd_scr[...] = ADAPTER_SCALING * mm_nt(grad_values, f3p[...])
         gd_scr[place, :] += ADAPTER_SCALING * mm_nt(grad_query, f1p[...])
-        grad_down = gd_scr[...].astype(BF)
-        gno_scr[...] = mm_nt(grad_keys, wa[1]) + mm_nt(grad_values, wa[2]) + mm(grad_down, f02[...])
-        gno_scr[place, :] += mm_nt(grad_query, wa[0])
-        gno_s[i] = gno_scr[...].astype(BF)
-
-        @pl.when(c != i // 2)
-        def _():
-            to_nbr(gno_s.at[i], gno_r.at[i % 2], 13 + i).start()
-
-        fg_a[...] += mm_tn(grad_down, n1[rows, :])[0:8]
+        fg_a[...] += mm_tn(gd_scr[...].astype(BF), n1[rows, :])[0:8]
         up_query = mm_tn(down[pl.ds(block_row[i], 128), :], grad_query)[0:8]
         up_value = mm_tn(down[rows, :], grad_values)[0:8]
         upper = lax.broadcasted_iota(jnp.int32, (8, 512), 0) < 4
         fg_b[...] += ADAPTER_SCALING * jnp.where(upper, up_query, up_value)
+
+    def rows_back(i):
+        rows = slice(256 * i, 256 * i + 256)
+        place = pl.ds(pl.multiple_of(128 * ((i + x) % 2), 128), 128)
+        gno_scr[...] = (
+            mm_nt(dk_acc[rows, :].astype(BF), wa[1])
+            + mm_nt(dv_acc[rows, :].astype(BF), wa[2])
+            + mm(gd_scr[...].astype(BF), f02[...])
+        )
+        gno_scr[place, :] += mm_nt(gq_scr[...], wa[0])
+        gno_s[i] = gno_scr[...].astype(BF)
+
+        @pl.when(c != i // 2)
+        def _():
+            to_nbr(gno_s.at[i], gno_r.at[i % 2], 13 + i).start()
+
+        def rows_sent():
+            @pl.when(c != i // 2)
+            def _():
+                to_nbr(gno_s.at[i], gno_r.at[i % 2], 13 + i).wait_send()
+
+        pending.append(rows_sent)
 
     def reduce_rows(i):
         @pl.when(c == i // 2)
@@ -686,65 +716,78 @@
             chip_s[i % 2] = (gno_s[i].astype(F32) + gno_r[i % 2].astype(F32)).astype(BF)
             to_owner(chip_s.at[i % 2], fin_r.at[x], i % 2, 24)
 
-    backward(3)
-    backward(2)
-    reduce_rows(3)
-    backward(1)
-    reduce_rows(2)
-    backward(0)
-    reduce_rows(1)
+        if i < 2:
+            pending.append(functools.partial(owner_sent, chip_s.at[i], fin_r.at[x], i, 24))
+
+    for i in (3, 2, 1):
+        scores_back(i)
+        factors_back(i)
+        rows_back(i)
+        if i < 3:
+            reduce_rows(i + 1)
+    scores_back(0)
+    factors_back(0)
 
     ps[0:8, :] = fg_a[...]
     for s in range(4):
         ps[8:16, pl.ds(column[s], 128)] = fg_b[:, 128 * s : 128 * s + 128]
-    to_nbr(ps, ps_r, 17).start()
-    reduce_rows(0)
+    send(to_nbr(ps, ps_r, 17))
+    rows_back(0)
     to_nbr(ps, ps_r, 17).wait_recv()
     mine = pl.ds(pl.multiple_of(8 * c, 8), 8)
     plane_buf[t] = ps[mine, :] + ps_r[mine, :]
-    copies = []
-    for k, device in enumerate(plane):
-        copies.append(remote(plane_buf.at[t], plane_buf.at[t], ssem.at[28 + k], rsem.at[28 + k], device))
-        copies[-1].start()
+    copies = [
+        remote(plane_buf.at[t], plane_buf.at[t], ssem.at[28 + k], rsem.at[28 + k], device)
+        for k, device in enumerate(plane)
+    ]
+    for copy in copies:
+        send(copy)
+    reduce_rows(1)
+    reduce_rows(0)
     for copy in copies:
         copy.wait_recv()
-    z_buf[z] = plane_buf[0] + plane_buf[1] + plane_buf[2] + plane_buf[3]
-    z_copies = []
+    z_buf[0] = plane_buf[0] + plane_buf[1] + plane_buf[2] + plane_buf[3]
     for k, device in enumerate(zs):
-        z_copies.append(remote(z_buf.at[z], z_buf.at[z], ssem.at[31 + k], rsem.at[31 + k], device))
-        z_copies[-1].start()
+        copy = remote(z_buf.at[2 * k], z_buf.at[2 * k + 1], ssem.at[31 + k], rsem.at[31 + k], device)
+        send(copy)
+        copy.wait_recv()
+        z_buf[2 * k + 2] = z_buf[2 * k] + z_buf[2 * k + 1]
+    fin[mine, :] = z_buf[2 * len(zs)]
+    send(to_nbr(fin.at[mine, :], fin.at[mine, :], 18))
+    theirs = pl.ds(pl.multiple_of(8 - 8 * c, 8), 8)
+    to_nbr(fin.at[theirs, :], fin.at[theirs, :], 18).wait_recv()
+    result = pltpu.make_async_copy(fin, summed, load_sem.at[0])
+    result.start()
 
     own_rows.wait()
     for first in (20, 22):
         for sender in range(2):
             place = pl.ds(128 * sender, 128)
-            remote(bo_s.at[pl.ds(0, 128), :], bo_r.at[place, :], ssem.at[first], rsem.at[first + sender], dests[0]).wait_recv()
-    block_out[...] = bo_r[...]
+            remote(
+                bo_s.at[pl.ds(0, 128), :], bo_r.at[place, :], ssem.at[first], rsem.at[first + sender], dests[0]
+            ).wait_recv()
     for sender in range(2):
         remote(chip_s.at[0], fin_r.at[sender], ssem.at[24], rsem.at[24 + sender], dests[0]).wait_recv()
-
-    @pl.loop(0, 2)
-    def _(r):
-        rows = pl.ds(pl.multiple_of(r * 128, 128), 128)
-        unit, inverse = unit_of(tokr[rows, :].astype(F32))
-        scaled = (fin_r[0, rows, :].astype(F32) + fin_r[1, rows, :].astype(F32)) * gain_one
-        input_grad[rows, :] = grf[rows, :].astype(F32) + inverse * (
-            scaled
-            - jnp.mean(scaled, -1, keepdims=True)
-            - unit * jnp.mean(scaled * unit, -1, keepdims=True)
-        )
-
-    for copy in z_copies:
-        copy.wait_recv()
-    total = z_buf[0]
-    for k in range(1, planes):
-        total = total + z_buf[k]
-    fin[mine, :] = total
-    to_nbr(fin.at[mine, :], fin.at[mine, :], 18).start()
-    theirs = pl.ds(pl.multiple_of(8 - 8 * c, 8), 8)
-    to_nbr(fin.at[theirs, :], fin.at[theirs, :], 18).wait_recv()
-
-    grad = fin[...]
+    result.wait()
+    drain()
+
+
+def finish_kernel(
+    norm_params, factors, first_moment, second_moment, bo_r, grf_in, fin_in, tok_in, sum_in,
+    block_out, input_grad, clipped, grad_norm, factors_new, first_new, second_new,
+    bo, grf, fin_r, tokr, summed, grads, sem, out_sem,
+):
+    pairs = [(sum_in, summed), (bo_r, bo)]
+    for r in range(2):
+        rows = pl.ds(128 * r, 128)
+        pairs += [(ref.at[rows, :], to.at[rows, :]) for ref, to in ((tok_in, tokr), (grf_in, grf))]
+        pairs.append((fin_in.at[:, rows, :], fin_r.at[:, rows, :]))
+    loads = [pltpu.make_async_copy(*pair, sem.at[k]) for k, pair in enumerate(pairs)]
+    for load in loads:
+        load.start()
+    loads[0].wait()
+
+    grad = summed[...]
     norm = jnp.sqrt(jnp.sum(grad * grad, (0, 1), keepdims=True))
     grad_norm[...] = norm
     grad = grad * (CLIP_NORM / jnp.maximum(norm, CLIP_NORM))
@@ -760,37 +803,32 @@
         factors_new[index] = weights - LEARN_RATE * (
             first_hat / (jnp.sqrt(second_hat) + ADAM_EPSILON) + WEIGHT_DECAY * weights
         )
-
-    @pl.when(c == y)
-    def _():
-        for item in doc:
-            to_nbr(*item).wait_send()
-
-    for slot in (1, 2, 3):
-        for group in range(GROUPS):
-            hop(slot, group).wait_send()
-    to_nbr(attn_s, attn_r, 8).wait_send()
-    to_nbr(n2.at[half, :], n2.at[half, :], 9).wait_send()
-    to_nbr(mlp_s, mlp_r, 10).wait_send()
-    to_nbr(gnt_s, gnt_r, 11).wait_send()
-    to_nbr(gr_b.at[half, :], gr_b.at[half, :], 12).wait_send()
-    to_nbr(ps, ps_r, 17).wait_send()
-    to_nbr(fin.at[mine, :], fin.at[mine, :], 18).wait_send()
-    for item in late:
-        owner_sent(*item)
-    for i in range(4):
-
-        @pl.when(c != i // 2)
-        def _():
-            to_nbr(gno_s.at[i], gno_r.at[i % 2], 13 + i).wait_send()
-
-    for j in range(2):
-        owner_sent(chip_s.at[j], fin_r.at[x], j, 24)
-    for copy in copies + z_copies:
-        copy.wait_send()
-
-
-def fused(planes, *args):
+    loads[1].wait()
+    stores = [pltpu.make_async_copy(bo, block_out, out_sem.at[2])]
+    stores[0].start()
+    for r in range(2):
+        for load in loads[2 + 3 * r : 5 + 3 * r]:
+            load.wait()
+        half = pl.ds(128 * r, 128)
+
+        @pl.loop(0, 2)
+        def _(q):
+            rows = pl.ds(pl.multiple_of(128 * r + q * 64, 64), 64)
+            unit, inverse = unit_of(tokr[rows, :].astype(F32))
+            scaled = (fin_r[0, rows, :].astype(F32) + fin_r[1, rows, :].astype(F32)) * norm_params[0:1, :]
+            grads[rows, :] = grf[rows, :].astype(F32) + inverse * (
+                scaled
+                - jnp.mean(scaled, -1, keepdims=True)
+                - unit * jnp.mean(scaled * unit, -1, keepdims=True)
+            )
+
+        stores.append(pltpu.make_async_copy(grads.at[half, :], input_grad.at[half, :], out_sem.at[r]))
+        stores[-1].start()
+    for store in stores:
+        store.wait()
+
+
+def fused(planes, tokens, norm_params, wqkv, w_out, w_fc, w_proj, factors, first, second, grad_out):
     vmem = pl.BlockSpec(memory_space=pltpu.VMEM)
     hbm = pl.BlockSpec(memory_space=pl.ANY)
 
@@ -807,31 +845,46 @@
         acc(512, 1024), buf(256, 1024), buf(256, 1024),
         acc(256, 1024), buf(512, 1024), acc(512, 1024), acc(512, 1024),
         buf(256, 1024), buf(256, 1024), buf(256, 1024), buf(256, 1024), buf(512, 1024),
-        buf(256, 1024), buf(256, 1024), buf(256, 1024),
+        buf(256, 1024),
         acc(1024, 512), acc(1024, 512), buf(128, 512), buf(4, 256, 512), acc(256, 1024),
-        buf(4, 256, 1024), buf(2, 256, 1024), buf(2, 256, 1024), buf(2, 256, 1024), buf(256, 1024),
+        buf(4, 256, 1024), buf(2, 256, 1024), buf(2, 256, 1024),
         acc(128, 1024), buf(128, 1024), buf(128, 512), buf(128, 512), buf(1024, 128), acc(256, 128),
-        acc(8, 1024), acc(8, 512), acc(16, 1024), acc(16, 1024), acc(4, 8, 1024), acc(planes, 8, 1024),
+        acc(8, 1024), acc(8, 512), acc(16, 1024), acc(16, 1024), acc(4, 8, 1024), acc(2 * planes, 8, 1024),
         acc(16, 1024),
         pltpu.SemaphoreType.DMA((3, GROUPS)), pltpu.SemaphoreType.DMA((3, GROUPS)),
         pltpu.SemaphoreType.DMA((9,)), pltpu.SemaphoreType.DMA((31 + planes,)),
         pltpu.SemaphoreType.DMA((31 + planes,)),
     ]
-    small = jax.ShapeDtypeStruct((4, 4, 1024), F32)
-    outs = pl.pallas_call(
+    rows = jax.ShapeDtypeStruct((256, 1024), BF)
+    passed = pl.pallas_call(
         functools.partial(fused_kernel, planes),
         name="block_step",
         out_shape=(
-            jax.ShapeDtypeStruct((256, 1024), BF), jax.ShapeDtypeStruct((256, 1024), F32), small,
-            jax.ShapeDtypeStruct((1, 1), F32), small, small, small,
+            rows, rows, jax.ShapeDtypeStruct((2, 256, 1024), BF), rows, jax.ShapeDtypeStruct((16, 1024), F32),
         ),
-        in_specs=[hbm, vmem, hbm, hbm, hbm, hbm, vmem, vmem, vmem, hbm],
-        out_specs=(vmem,) * 7,
+        in_specs=[hbm, vmem, hbm, hbm, hbm, hbm, vmem, hbm],
+        out_specs=(hbm,) * 5,
         scratch_shapes=scratch,
         compiler_params=pltpu.CompilerParams(
             collective_id=1, has_side_effects=True, vmem_limit_bytes=62 << 20
         ),
-    )(*args)
+    )(tokens, norm_params, wqkv, w_out, w_fc, w_proj, factors, grad_out)
+    small = jax.ShapeDtypeStruct((4, 4, 1024), F32)
+    outs = pl.pallas_call(
+        finish_kernel,
+        name="finish_step",
+        out_shape=(
+            rows, jax.ShapeDtypeStruct((256, 1024), F32), small,
+            jax.ShapeDtypeStruct((1, 1), F32), small, small, small,
+        ),
+        in_specs=[vmem] * 4 + [hbm] * 5,
+        out_specs=(hbm, hbm) + (vmem,) * 5,
+        scratch_shapes=[
+            buf(256, 1024), buf(256, 1024), buf(2, 256, 1024), buf(256, 1024), acc(16, 1024), acc(256, 1024),
+            pltpu.SemaphoreType.DMA((8,)), pltpu.SemaphoreType.DMA((3,)),
+        ],
+        compiler_params=pltpu.CompilerParams(vmem_limit_bytes=62 << 20),
+    )(norm_params, factors, first, second, *passed)
     return outs[:3] + (outs[3].reshape(()),) + outs[4:]
 
 

time: 146 us -> 135 us (0.925)
  local copies, waits for them, and re-layouts: 6.77 us -> 0 us
  Pallas kernels: 137 us -> 134 us
  between operations: 2.37 us -> 0.8 us
    pallas_call x1, Pallas kernels: 137 us -> 129 us  [fused(): pl.pallas_call(functools.partial(fused_kernel, planes), name='block_step'...]
    unnamed x14 -> x0, local copies, waits for them, and re-layouts: 6.77 us -> none
    pallas_call x0 -> x1, Pallas kernels: none -> 5.14 us  [fused(): pl.pallas_call(finish_kernel, name='finish_step', out_shape=(rows, jax.Sh...]
where the time goes in v2:
time: 135 us
  Pallas kernels  134 us (99%)
    pallas_call x1, Pallas kernels, fused(): pl.pallas_call(functools.partial(fused_kernel, planes), name='block_step'...  129 us
    pallas_call x1, Pallas kernels, fused(): pl.pallas_call(finish_kernel, name='finish_step', out_shape=(rows, jax.Sh...  5.14 us

profile of v2, /device:TPU:1, one launch (start us, length us, event | category | flops | bytes accessed | tf_op | source)
XLA Modules:
  0.0 135.2 jit_solution(17076648383097495137)
XLA Ops:
  0.6 129.3 %block_step.1 = (bf16[256,1024]{1,0:T(8,128)(2,1)}, bf16[256,1024]{1,0:T(8,128)(2,1)}, bf16[2,256,1024]{2,1,0:T(8,128)(2,1)}, bf16[256,1024]{1,0:T(8,128)(2,1)}, f32[16,1024]{1,0:T(8,128)}) custom-call(bf16[1024,1024]{1,0:T(8,128)(2,1)} %tokens.1, f32[4,1024]{1,0:T(4,128)} %norm_params.3, bf16[3,1024,256]{2,1,0:T(8,128)(2,1)} %wqkv.1, ...), custom_call_target="tpu_custom_call" | custom-call | tf_op jit(solution)/shard_map/block_step/pallas_call | solution.py:859
  129.9 5.1 %finish_step.1 = (bf16[256,1024]{1,0:T(8,128)(2,1)}, f32[256,1024]{1,0:T(8,128)}, f32[4,4,1024]{2,1,0:T(4,128)}, f32[1,1]{1,0:T(1,128)}, f32[4,4,1024]{2,1,0:T(4...) custom-call(f32[4,1024]{1,0:T(4,128)} %norm_params.3, f32[4,4,1024]{2,1,0:T(4,128)} %factors.3, ...), custom_call_target="tpu_custom_call" | custom-call | tf_op jit(solution)/shard_map/finish_step/pallas_call | solution.py:873
